TPU v7x, 256 devices: a whole 4x4x8 slice. The times are simulated.
256 devices in a mesh: dp: 32 (over x, y, core), mp: 8 (over z).
Axes of the slice: x: 4, y: 4, z: 8, core: 2. Of those that a mesh axis runs over, the one named last changes fastest.
Arguments:
- payload: bfloat16 [32, 512, 2, 10240], P('dp', None, None, 'mp'), may hold values from -6 to 6
- block_scale: float32 [32, 512, 2, 80], P('dp', None, None, 'mp'), may hold values from 0.25 to 4
- master: float32 [512, 2, 10240], P('dp', None, 'mp'), may hold values from -0.0006 to 0.0006
- moment_one: float32 [512, 2, 10240], P('dp', None, 'mp'), may hold values from -12 to 12
- moment_two: float32 [512, 2, 10240], P('dp', None, 'mp'), may hold values from 4 to 100
- owner: int32 [512, 1], P('dp'), may hold values from 0 to 31; in each aligned block of 16 rows (0 to 15, 16 to 31, ...) at most 2 rows name the same one
Outputs:
- new_master: float32 [512, 2, 10240], P('dp', None, 'mp')
- new_moment_one: float32 [512, 2, 10240], P('dp', None, 'mp')
- new_moment_two: float32 [512, 2, 10240], P('dp', None, 'mp')
- next_rows: bfloat16 [2048, 2, 10240], P(('dp', 'mp'))
Inputs may be any that keep to these rules, and one draw needn't show every extreme that they name: Among the 16 rows of one device at most 2 name the same owner, and in every draw some device has exactly 2 rows naming one owner.
All inputs are finite; a program needn't handle non-finite values.
Results may differ from a plain program's by a relative error of at most 0.015.
Values may be sent and summed in bfloat16 or wider, within the bound.
A program may use at most 64 MiB of HBM per device.

v0:
```python
import jax
import jax.numpy as jnp
from jax import lax
from jax.sharding import PartitionSpec as P

BLOCK = 128
STEP = 100


def dequantize(values, scales):
    shape = values.shape
    blocks = values.astype(jnp.float32).reshape(shape[:-1] + (scales.shape[-1], BLOCK))
    return (blocks * scales[..., None]).reshape(shape)


def body(payload, block_scale, master, moment_one, moment_two, owner):
    row_count = master.shape[0]
    values = payload[0]
    scales = block_scale[0]
    grad = lax.psum_scatter(
        dequantize(values, scales).astype(jnp.bfloat16), "dp", scatter_dimension=0, tiled=True
    ).astype(jnp.float32)
    step_count = STEP + 1
    new_moment_one = 0.9 * moment_one + 0.1 * grad
    new_moment_two = 0.95 * moment_two + 0.05 * grad * grad
    first_fix = 1.0 - 0.9**step_count
    second_fix = 1.0 - 0.95**step_count
    direction = new_moment_one / first_fix / (jnp.sqrt(new_moment_two / second_fix) + 1e-08)
    new_master = master - 0.00015 * (direction + 0.1 * master)
    rounded = new_master.astype(jnp.bfloat16).reshape(row_count, -1)
    replicas = lax.axis_size("dp")
    capacity = max(2, 2 * row_count // replicas)
    slot_total = replicas * capacity
    targets = owner[:, 0]
    same = targets[:, None] == targets[None, :]
    earlier = jnp.arange(row_count)[:, None] > jnp.arange(row_count)[None, :]
    rank = jnp.sum((same & earlier).astype(jnp.int32), axis=1)
    slot_index = targets * capacity + rank
    select = (slot_index[None, :] == jnp.arange(slot_total, dtype=jnp.int32)[:, None]).astype(
        jnp.bfloat16
    )
    outgoing = jnp.dot(select, rounded, preferred_element_type=jnp.float32).astype(jnp.bfloat16)
    outgoing = outgoing.reshape(slot_total, master.shape[1], master.shape[2])
    next_rows = lax.all_to_all(
        lax.all_to_all(outgoing, "dp", split_axis=0, concat_axis=0, tiled=True),
        "mp",
        split_axis=0,
        concat_axis=2,
        tiled=True,
    )
    return (new_master, new_moment_one, new_moment_two, next_rows)


def solution(mesh):
    return jax.shard_map(
        body,
        mesh=mesh,
        in_specs=(
            P("dp", None, None, "mp"),
            P("dp", None, None, "mp"),
            P("dp", None, "mp"),
            P("dp", None, "mp"),
            P("dp", None, "mp"),
            P("dp", None),
        ),
        out_specs=(
            P("dp", None, "mp"),
            P("dp", None, "mp"),
            P("dp", None, "mp"),
            P(("dp", "mp"), None, None),
        ),
        check_vma=False,
    )
```

profile of v0, /device:TPU:1, one launch (start us, length us, event | category | flops | bytes accessed | tf_op | source)
XLA Modules:
  0.0 190.4 jit_solution(12685848988058559482)
XLA Ops:
  7.2 0.0 copy-start.3
  7.2 0.0 all-reduce.3.cloned.1.call-start
  7.2 7.4 %copy.29 = bf16[1,512,2,1280]{1,3,2,0:T(8,128)(2,1)} copy(bf16[1,512,2,1280]{3,2,1,0:T(2,128)(2,1)} %param.6) | data formatting | bytes 5242880 | tf_op args[0]
  14.6 0.0 copy-done.3
  14.6 2.2 %fusion = bf16[512,2,1280]{0,2,1:T(8,128)(2,1)S(1)} fusion(bf16[1,512,2,1280]{1,3,2,0:T(8,128)(2,1)} %copy.29, f32[512,2,10]{0,2,1:T(8,128)S(1)} %copy.30), kind=kLoop, calls=%fused_computation.1 | loop fusion | flops 3932160 | bytes 5283840 | tf_op jit(solution)/shard_map/convert_element_type | solution.py:21
  16.9 4.8 %copy.31 = bf16[512,2,1280]{2,1,0:T(2,128)(2,1)} copy(bf16[512,2,1280]{0,2,1:T(8,128)(2,1)S(1)} %fusion) | data formatting | bytes 5242880 | tf_op jit(solution)/shard_map/convert_element_type | solution.py:21
  21.7 0.0 copy-start.5
  21.7 0.0 copy-start.4
  21.7 0.0 copy-start
  21.7 0.0 copy-start.1
  21.7 0.0 copy-start.2
  21.7 0.0 all-reduce.3.cloned.1.call-update
  21.8 0.6 copy-done.5
  22.4 0.6 dynamic-slice
  23.6 0.0 copy-done.4
  23.6 0.2 convert_reduce_fusion
  23.8 120.5 %all-reduce.3.cloned.1.call-done = bf16[512,2,1280]{2,1,0:T(2,128)(2,1)} async-done(((bf16[512,2,1280]{2,1,0:T(2,128)(2,1)}), bf16[512,2,1280]{2,1,0:T(2,128)(2,1)}) %all-reduce.3.cloned.1.call-update) | async-done | bytes 2621456
  144.3 0.0 copy-done
  144.3 0.0 copy-done.1
  144.3 0.0 copy-done.2
  144.3 2.2 %fusion.5 = (bf16[16,2,1280]{2,1,0:T(2,128)(2,1)S(1)}, f32[16,2,1280]{2,1,0:T(2,128)}, f32[16,2,1280]{2,1,0:T(2,128)}, f32[16,2,1280]{2,1,0:T(2,128)}) fusion(f32[16,2,1280]{2,1,0:T(2,128)S(1)} %copy-done, bf16[512,2,1280]{2,1,0:T(2,128)(2,1)} %all-reduce.3.cloned.1.call-done, u32[]{:T(128)S(6)} %multiply.3, f32[16,2,1280]{2,1,0:T(2,128)S(1)} %copy-done.1, ...), kind=kLoop, calls=%fused_computation.15 | loop fusion | flops 696320 | bytes 1146884 | tf_op jit(solution)/shard_map/convert_element_type | solution.py:30
  146.5 0.2 convolution_convert_fusion
  146.7 0.1 reshape.32
  146.8 15.5 %all_to_all.23 = bf16[64,2,1280]{2,1,0:T(2,128)(2,1)S(1)} all-to-all(bf16[64,2,1280]{2,1,0:T(2,128)(2,1)S(1)} %reshape.32), channel_id=1, replica_groups=mesh['dp'=32,'mp'=8] {'dp'}, dimensions={0} | all-to-all | bytes 655360 | tf_op jit(solution)/shard_map/all_to_all | solution.py:45
  162.3 20.3 %all_to_all.24 = bf16[64,2,1280]{2,1,0:T(2,128)(2,1)S(1)} all-to-all(bf16[64,2,1280]{2,1,0:T(2,128)(2,1)S(1)} %all_to_all.23), channel_id=1, replica_groups=mesh['dp'=32,'mp'=8] {'mp'}, dimensions={0} | all-to-all | bytes 655360 | tf_op jit(solution)/shard_map/all_to_all | solution.py:44
  182.6 0.1 copy.35
  182.7 0.8 all_to_all.20
  (3 shorter events, 0.0 us)
Async XLA Ops:
  7.2 7.4 %copy-start.3 = (f32[1,512,2,10]{1,2,3,0:T(2,128)S(1)}, f32[1,512,2,10]{1,2,3,0:T(2,128)}, u32[]{:S(2)}) copy-start(f32[1,512,2,10]{1,2,3,0:T(2,128)} %param.7) | copy-start | bytes 122884
  7.2 137.1 %all-reduce.3.cloned.1.call-start = ((), (), s32[]{:S(2)}) async-start(), calls=%async_computation.2 | async-start | bytes 5242880
  21.7 0.7 copy-start.5
  21.7 1.9 %copy-start.4 = (s32[16,1]{0,1:T(1,128)S(1)}, s32[16,1]{0,1:T(1,128)}, u32[]{:S(2)}) copy-start(s32[16,1]{0,1:T(1,128)} %param.11) | copy-start | bytes 196
  21.7 122.6 %copy-start = (f32[16,2,1280]{2,1,0:T(2,128)S(1)}, f32[16,2,1280]{2,1,0:T(2,128)}, u32[]{:S(2)}) copy-start(f32[16,2,1280]{2,1,0:T(2,128)} %param.8) | copy-start | bytes 491524
  21.7 122.6 %copy-start.1 = (f32[16,2,1280]{2,1,0:T(2,128)S(1)}, f32[16,2,1280]{2,1,0:T(2,128)}, u32[]{:S(2)}) copy-start(f32[16,2,1280]{2,1,0:T(2,128)} %param.9) | copy-start | bytes 491524
  21.7 122.6 %copy-start.2 = (f32[16,2,1280]{2,1,0:T(2,128)S(1)}, f32[16,2,1280]{2,1,0:T(2,128)}, u32[]{:S(2)}) copy-start(f32[16,2,1280]{2,1,0:T(2,128)} %param.10) | copy-start | bytes 491524
Sparse Core Ops, SparseCore 0:
  21.9 122.3 all-reduce.2
where the time goes:
time: 191 us; the launch traced here: 190 us
  waiting for transfers between devices  120 us (63%)
  blocking collectives  35.8 us (19%)
  between operations  14.8 us (8%)
  local copies, waits for them, and re-layouts  14.4 us (8%)
  other arithmetic  4.66 us (2%)
    unnamed x2, waiting for transfers between devices  120 us
    all_to_all x1, blocking collectives, body(): lax.all_to_all(lax.all_to_all(outgoing, 'dp', split_axis=0, concat_axis=0...  20.3 us
    all_to_all x1, blocking collectives, body(): lax.all_to_all(outgoing, 'dp', split_axis=0, concat_axis=0, tiled=True)  15.5 us
    unnamed x15, local copies, waits for them, and re-layouts  8.62 us
    convert_element_type x1, local copies, waits for them, and re-layouts, body(): dequantize(values, scales).astype(jnp.bfloat16)  4.83 us
  transfers between devices with their start and end apart: 1, of which 1 were waited for; matrix products, arithmetic and copies ran while one was open for 0% of the time, Pallas kernels for 0%

commit v1 on v0

v1 whole, which is shorter than its diff:
```python
import jax
import jax.numpy as jnp
from jax import lax
from jax.experimental import pallas as pl
from jax.experimental.pallas import tpu as pltpu
from jax.sharding import PartitionSpec as P

STEP = 100
ROWS = 16
TILES = 10
SIDE = 4
DEPTH = 8
NDP = 32
KEYS = 64
MESH = pl.DeviceIdType.MESH
BF16 = jnp.bfloat16
F32 = jnp.float32
GROUPS = ((0, 0, 5), (1, 5, 5))
CHUNKS = ((0, 10, (0, 1)),)
OFFSETS = (2, 1, 3, 0)


def iota(shape, dim):
    return lax.broadcasted_iota(jnp.int32, shape, dim)


def scratch():
    made = {
        "pay": pltpu.VMEM((NDP, TILES, ROWS, 2, 128), BF16),
        "scale": pltpu.VMEM((TILES, 2, 512), F32),
        "keys": pltpu.VMEM((2 * NDP * ROWS, KEYS), BF16),
        "state_in": pltpu.VMEM((3, TILES, ROWS, 2, 128), F32),
        "state": pltpu.VMEM((3, TILES, 32, 128), F32),
        "fresh": pltpu.VMEM((3, TILES, 32, 128), F32),
        "rounded": pltpu.VMEM((TILES, 32, 128), BF16),
        "owner": pltpu.VMEM((1, ROWS), jnp.int32),
        "load_sem": pltpu.SemaphoreType.DMA((TILES,)),
        "scale_sem": pltpu.SemaphoreType.DMA((2,)),
        "state_sem": pltpu.SemaphoreType.DMA((3, TILES)),
        "fresh_sem": pltpu.SemaphoreType.DMA,
    }
    for g, (_, _, n) in enumerate(GROUPS):
        block = (n, 32, 128)
        made |= {
            f"give{g}": pltpu.VMEM((SIDE, SIDE) + block, BF16),
            f"take{g}": pltpu.VMEM((SIDE, SIDE) + block, BF16),
            f"own{g}": pltpu.VMEM((SIDE, SIDE) + block, F32),
            f"first{g}": pltpu.VMEM((3, SIDE) + block, BF16),
            f"first_in{g}": pltpu.VMEM((3, SIDE) + block, BF16),
            f"second{g}": pltpu.VMEM((3,) + block, BF16),
            f"second_in{g}": pltpu.VMEM((3,) + block, BF16),
            f"total{g}": pltpu.VMEM(block, F32),
            f"pair_sem{g}": pltpu.SemaphoreType.DMA((2, 4)),
            f"first_sem{g}": pltpu.SemaphoreType.DMA((2, 3)),
            f"second_sem{g}": pltpu.SemaphoreType.DMA((2, 3)),
        }
    for h, (_, n, _) in enumerate(CHUNKS):
        made |= {
            f"select{h}": pltpu.VMEM((128 * n, 32 * n), BF16),
            f"slots{h}": pltpu.VMEM((NDP, 4 * n, 128), BF16),
            f"plane{h}": pltpu.VMEM((DEPTH, 4, 4 * n, 128), BF16),
            f"plane_sem{h}": pltpu.SemaphoreType.DMA((2, NDP)),
            f"deep_sem{h}": pltpu.SemaphoreType.DMA((2, DEPTH)),
        }
    return made


NAMES = tuple(scratch())


def kernel(pay_in, scale_in, master_in, one_in, two_in, owner_in, *rest):
    fresh_out, next_out = rest[0], rest[1:1 + len(CHUNKS)]
    r = dict(zip(NAMES, rest[1 + len(CHUNKS):]))
    dp, z = lax.axis_index("dp"), lax.axis_index("mp")
    c, y, x = dp % 2, dp // 2 % SIDE, dp // (2 * SIDE)

    def place(px, py, pc):
        return (px * SIDE + py) * 2 + pc

    def signal(device):
        pl.semaphore_signal(barrier, inc=1, device_id=device, device_id_type=MESH)

    def remote(src, dst, sems, i, j, device):
        return pltpu.make_async_remote_copy(
            src, dst, sems.at[0, i], sems.at[1, j], device_id=device, device_id_type=MESH
        )

    barrier = pltpu.get_barrier_semaphore()

    def greet_plane(i, carry):
        signal(((dp + i) % NDP, z))
        return carry

    def greet_depth(i, carry):
        signal((dp, (z + i) % DEPTH))
        return carry

    lax.fori_loop(1, NDP, greet_plane, 0)
    lax.fori_loop(1, DEPTH, greet_depth, 0)

    scale_load = pltpu.make_async_copy(scale_in, r["scale"], r["scale_sem"].at[0])
    owner_load = pltpu.make_async_copy(owner_in, r["owner"], r["scale_sem"].at[1])
    loads = [
        pltpu.make_async_copy(pay_in.at[:, :, t], r["pay"].at[:, t], r["load_sem"].at[t])
        for t in range(TILES)
    ]
    state_loads = [
        pltpu.make_async_copy(ref.at[:, t], r["state_in"].at[i, t], r["state_sem"].at[i, t])
        for i, ref in enumerate((master_in, one_in, two_in))
        for t in range(TILES)
    ]
    for copy in [scale_load, owner_load] + loads + state_loads:
        copy.start()

    scale_load.wait()
    spread = (iota((256, 128), 0) // 2 == iota((256, 128), 1)).astype(BF16)
    match = iota((256, KEYS), 0) % 2 == iota((256, KEYS), 1) // 10 % 2

    for k in range(4):
        whole = [r["scale"][:, i, 128 * k : 128 * k + 128] for i in range(2)]
        parts = []
        for _ in range(3):
            part = [value.astype(BF16).astype(F32) for value in whole]
            whole = [value - near for value, near in zip(whole, part)]
            parts += part
        parts = jnp.concatenate(parts + [jnp.zeros((KEYS - 60, 128), F32)], axis=0)
        turned = lax.dot_general(
            spread, parts.astype(BF16), (((1,), (1,)), ((), ())), preferred_element_type=F32
        )
        r["keys"][256 * k : 256 * k + 256, :] = jnp.where(match, turned, 0.0).astype(BF16)

    owner_load.wait()
    targets = r["owner"][...].astype(F32)
    square = (ROWS, ROWS)
    diagonal = jnp.where(iota(square, 0) == iota(square, 1), jnp.broadcast_to(targets, square), 0.0)
    columns = jnp.dot(diagonal.astype(BF16), jnp.ones(square, BF16), preferred_element_type=F32)
    earlier = (columns == targets) & (iota(square, 0) < iota(square, 1))
    rank = jnp.sum(jnp.where(earlier, 1.0, 0.0), axis=0, keepdims=True)
    slot = jnp.broadcast_to(targets * 2.0 + rank, (8, ROWS)).astype(BF16)
    for h, (_, n, _) in enumerate(CHUNKS):
        wide = (ROWS, 32 * n)
        repeat = (iota(wide, 1) % 32 // 2 == iota(wide, 0)).astype(BF16)
        slots = jnp.dot(slot, repeat, preferred_element_type=F32)[0:1]
        line = iota((1, 32 * n), 1)
        goal = slots.astype(jnp.int32) * (2 * n) + line // 32 * 2 + line % 2
        r[f"select{h}"][...] = (iota((128 * n, 32 * n), 0) == goal).astype(BF16)

    for copy in loads:
        copy.wait()
    centre = ((x, y), (y, x))

    def block_of(g, a, b, core):
        return place(a, b, core) if GROUPS[g][0] == 0 else place(b, a, core)

    widen = []
    for _, t0, n in GROUPS:
        shape = (KEYS, 128 * n)
        widen.append((iota(shape, 0) % 10 == iota(shape, 1) // 128 + t0).astype(BF16))

    def terms(g, a, b, core):
        _, t0, n = GROUPS[g]
        block = block_of(g, a, b, core)
        keys = r["keys"][pl.ds(pl.multiple_of(32 * block, 32), 32), :]
        scales = jnp.dot(keys, widen[g], preferred_element_type=F32)
        for t in range(n):
            values = r["pay"][block, t0 + t].reshape(32, 128).astype(F32)
            yield t, values * scales[:, 128 * t : 128 * t + 128]

    for g in range(len(GROUPS)):

        def give(i, carry, g=g):
            a, b = i // SIDE, i % SIDE
            for t, term in terms(g, a, b, 1 - c):
                r[f"give{g}"][a, b, t] = term.astype(BF16)
            return carry

        lax.fori_loop(0, SIDE * SIDE, give, 0)
    for g in range(len(GROUPS)):

        def keep(i, carry, g=g):
            a, b = i // SIDE, i % SIDE
            for t, term in terms(g, a, b, c):
                r[f"own{g}"][a, b, t] = term
            return carry

        lax.fori_loop(0, SIDE * SIDE, keep, 0)

    for copy in state_loads:
        copy.wait()

    def turn(t, carry):
        for i in range(3):
            r["state"][i, t] = r["state_in"][i, t].reshape(32, 128)
        return carry

    lax.fori_loop(0, TILES, turn, 0)
    pl.semaphore_wait(barrier, NDP - 1 + DEPTH - 1)

    pair = {}
    for k in range(4):
        for g, (axis, _, _) in enumerate(GROUPS):
            a = (centre[axis][0] + OFFSETS[k]) % SIDE
            pair[g, k] = remote(
                r[f"give{g}"].at[a],
                r[f"take{g}"].at[a],
                r[f"pair_sem{g}"],
                k,
                k,
                (place(x, y, 1 - c), z),
            )
            pair[g, k].start()
    first = {}
    for k in range(4):
        for g, (axis, _, n) in enumerate(GROUPS):
            a = (centre[axis][0] + OFFSETS[k]) % SIDE
            pair[g, k].wait_recv()

            def add(b, carry, g=g, n=n, k=k, a=a):
                for t in range(n):
                    total = r[f"own{g}"][a, b, t] + r[f"take{g}"][
                        a, b, t
                    ].astype(F32)
                    if k < 3:
                        r[f"first{g}"][k, b, t] = total.astype(BF16)
                    else:
                        r[f"own{g}"][a, b, t] = total
                return carry

            lax.fori_loop(0, SIDE, add, 0)
            if k < 3:
                there = place(a, y, c) if axis == 0 else place(x, a, c)
                first[g, k] = remote(
                    r[f"first{g}"].at[k], r[f"first_in{g}"].at[k], r[f"first_sem{g}"], k, k, (there, z)
                )
                first[g, k].start()
    second = {}
    for g, (axis, _, n) in enumerate(GROUPS):
        a, b0 = centre[axis]
        for k in range(3):
            first[g, k].wait_recv()
        for k in range(4):
            b = (b0 + OFFSETS[k]) % SIDE
            for t in range(n):
                total = r[f"own{g}"][a, b, t]
                for j in range(3):
                    total += r[f"first_in{g}"][j, b, t].astype(F32)
                if k < 3:
                    r[f"second{g}"][k, t] = total.astype(BF16)
                else:
                    r[f"total{g}"][t] = total
            if k < 3:
                there = place(x, b, c) if axis == 0 else place(b, y, c)
                second[g, k] = remote(
                    r[f"second{g}"].at[k],
                    r[f"second_in{g}"].at[k],
                    r[f"second_sem{g}"],
                    k,
                    k,
                    (there, z),
                )
                second[g, k].start()
    stores = []
    fix_one = 1.0 - 0.9 ** (STEP + 1)
    fix_two = 1.0 - 0.95 ** (STEP + 1)
    for h, (h0, hn, members) in enumerate(CHUNKS):
        for g in members:
            _, t0, n = GROUPS[g]
            for k in range(3):
                second[g, k].wait_recv()
            for t in range(n):
                grad = r[f"total{g}"][t]
                for j in range(3):
                    grad += r[f"second_in{g}"][j, t].astype(F32)
                master, one, two = (
                    r["state"][i, t0 + t] for i in range(3)
                )
                one = 0.9 * one + 0.1 * grad
                two = 0.95 * two + 0.05 * grad * grad
                direction = one / fix_one / (jnp.sqrt(two / fix_two) + 1e-08)
                master = master - 0.00015 * (direction + 0.1 * master)
                for i, value in enumerate((master, one, two)):
                    r["fresh"][i, t0 + t] = value
                r["rounded"][t0 + t] = master.astype(BF16)
        rows = r["rounded"][h0 : h0 + hn].reshape(32 * hn, 128)
        moved = jnp.dot(r[f"select{h}"][...], rows, preferred_element_type=F32)
        r[f"slots{h}"][...] = moved.reshape(NDP, 4 * hn, 128).astype(BF16)

        def send(i, carry, h=h):
            d = (dp + i) % NDP
            remote(
                r[f"slots{h}"].at[d], r[f"plane{h}"].at[dp // 4, dp % 4], r[f"plane_sem{h}"], i, i, (d, z)
            ).start()
            return carry

        lax.fori_loop(1, NDP, send, 0)
        stay = pltpu.make_async_copy(
            r[f"slots{h}"].at[dp], r[f"plane{h}"].at[dp // 4, dp % 4], r[f"plane_sem{h}"].at[0, 0]
        )
        stay.start()
        def land(i, carry, h=h):
            d = (dp + NDP - i) % NDP
            remote(
                r[f"slots{h}"].at[d], r[f"plane{h}"].at[d // 4, d % 4], r[f"plane_sem{h}"], i, i, (d, z)
            ).wait_recv()
            return carry

        lax.fori_loop(1, NDP, land, 0)
        stay.wait()
    copy = pltpu.make_async_copy(r["fresh"], fresh_out, r["fresh_sem"])
    copy.start()
    stores.append(copy)
    deep, own = [], []
    for h, (h0, hn, _) in enumerate(CHUNKS):
        there = next_out[h].at[z]
        grouped = r[f"plane{h}"]
        for i in (4, 3, 5, 2, 6, 1, 7):
            to = (z + i) % DEPTH
            copy = remote(grouped.at[to], there, r[f"deep_sem{h}"], i, i, (dp, to))
            copy.start()
            deep.append(copy)
        copy = pltpu.make_async_copy(grouped.at[z], there, r[f"deep_sem{h}"].at[0, 0])
        copy.start()
        own.append(copy)
    for copy in list(pair.values()) + list(first.values()) + list(second.values()):
        copy.wait_send()
    for h in range(len(CHUNKS)):

        def sent(i, carry, h=h):
            d = (dp + i) % NDP
            remote(
                r[f"slots{h}"].at[d], r[f"plane{h}"].at[dp // 4, dp % 4], r[f"plane_sem{h}"], i, i, (d, z)
            ).wait_send()
            return carry

        lax.fori_loop(1, NDP, sent, 0)
    for copy in stores + own + deep:
        copy.wait()


def finish(fresh, *rest):
    parts = len(CHUNKS)
    arrived, outs, rows_out = rest[:parts], rest[parts : parts + 3], rest[parts + 3]
    state, state_in_sem, state_sem, rows_in_sem, rows_sem = rest[parts + 4 : parts + 9]
    rows = rest[parts + 9 :]
    loads = [pltpu.make_async_copy(fresh, state, state_in_sem)]
    loads += [pltpu.make_async_copy(arrived[h], rows[h], rows_in_sem.at[h]) for h in range(parts)]
    for copy in loads:
        copy.start()
    copies = []

    def store(src, dst, sem):
        copies.append(pltpu.make_async_copy(src, dst, sem))
        copies[-1].start()

    loads[0].wait()
    for i in range(3):
        for t in range(TILES):
            store(state.at[i, t], outs[i].at[:, t], state_sem.at[i, t])
    for h, (h0, n, _) in enumerate(CHUNKS):
        loads[1 + h].wait()
        for m in range(DEPTH):
            store(rows[h].at[m], rows_out.at[:, pl.ds(m * TILES + h0, n)], rows_sem.at[h, m])
    for copy in copies:
        copy.wait()


def body(payload, block_scale, master, moment_one, moment_two, owner):
    def fold(array):
        split = array.shape[:-1] + (array.shape[-1] // 128, 128)
        return jnp.swapaxes(array.reshape(split), -3, -2)

    def unfold(array):
        array = jnp.swapaxes(array, -3, -2)
        return array.reshape(array.shape[:-2] + (-1,))

    anywhere = pl.BlockSpec(memory_space=pl.ANY)
    fresh, *arrived = pl.pallas_call(
        kernel,
        out_shape=(
            jax.ShapeDtypeStruct((3, TILES, 32, 128), F32),
            *(jax.ShapeDtypeStruct((DEPTH, 4, 4 * n, 128), BF16) for _, n, _ in CHUNKS),
        ),
        in_specs=[anywhere] * 6,
        out_specs=(anywhere,) * (1 + len(CHUNKS)),
        scratch_shapes=list(scratch().values()),
        compiler_params=pltpu.CompilerParams(
            collective_id=0, has_side_effects=True, vmem_limit_bytes=60 * 2**20
        ),
    )(
        fold(payload[0].reshape(NDP, ROWS, 2, -1)),
        jnp.transpose(block_scale[0], (2, 1, 0)),
        fold(master),
        fold(moment_one),
        fold(moment_two),
        owner.T,
    )
    state = jax.ShapeDtypeStruct((ROWS, TILES, 2, 128), F32)
    results = pl.pallas_call(
        finish,
        out_shape=(state, state, state, jax.ShapeDtypeStruct((8, DEPTH * TILES, 2, 128), BF16)),
        in_specs=[anywhere] * (1 + len(CHUNKS)),
        out_specs=(anywhere,) * 4,
        scratch_shapes=[
            pltpu.VMEM((3, TILES, ROWS, 2, 128), F32),
            pltpu.SemaphoreType.DMA,
            pltpu.SemaphoreType.DMA((3, TILES)),
            pltpu.SemaphoreType.DMA((len(CHUNKS),)),
            pltpu.SemaphoreType.DMA((len(CHUNKS), DEPTH)),
            *(pltpu.VMEM((DEPTH, 8, n, 2, 128), BF16) for _, n, _ in CHUNKS),
        ],
    )(
        fresh.reshape(3, TILES, ROWS, 2, 128),
        *(part.reshape(DEPTH, 8, n, 2, 128) for part, (_, n, _) in zip(arrived, CHUNKS)),
    )
    return tuple(unfold(result) for result in results)


def solution(mesh):
    return jax.shard_map(
        body,
        mesh=mesh,
        in_specs=(
            P("dp", None, None, "mp"),
            P("dp", None, None, "mp"),
            P("dp", None, "mp"),
            P("dp", None, "mp"),
            P("dp", None, "mp"),
            P("dp", None),
        ),
        out_specs=(
            P("dp", None, "mp"),
            P("dp", None, "mp"),
            P("dp", None, "mp"),
            P(("dp", "mp"), None, None),
        ),
        check_vma=False,
    )
```

time: 191 us -> 56.2 us (0.29)
  waiting for transfers between devices: 120 us -> 0 us
  Pallas kernels: 0 us -> 55.4 us
  blocking collectives: 35.8 us -> 0 us
  local copies, waits for them, and re-layouts: 14.4 us -> 0 us
  between operations: 14.8 us -> 0.64 us
  other arithmetic: 4.66 us -> 0 us
    unnamed x2 -> x0, waiting for transfers between devices: 120 us -> none
    pallas_call x0 -> x2, Pallas kernels: none -> 55.4 us  [the longest x1 53.2 us: body(): pl.pallas_call(kernel, out_shape=(jax.ShapeDtypeStruct((3, TILES, 32, 128...]
    all_to_all x2 -> x0, blocking collectives: 35.8 us -> none  [the longest x1 20.3 us: body(): lax.all_to_all(lax.all_to_all(outgoing, 'dp', split_axis=0, concat_axis=0...]
    unnamed x15 -> x0, local copies, waits for them, and re-layouts: 8.62 us -> none
    convert_element_type x1 -> x0, local copies, waits for them, and re-layouts: 4.83 us -> none  [body(): dequantize(values, scales).astype(jnp.bfloat16)]
    convert_element_type x2 -> x0, other arithmetic: 4.47 us -> none  [the longest x1 2.25 us: body(): dequantize(values, scales).astype(jnp.bfloat16)]
  transfers between devices with their start and end apart: 1 -> 0, of which waited for: 1 -> 0; matrix products, arithmetic and copies ran while one was open for 0% -> 0% of each run, Pallas kernels for 0% -> 0%
where the time goes in v1:
time: 56.2 us; the launch traced here: 56.1 us
  Pallas kernels  55.4 us (99%)
  between operations  0.64 us (1%)
    pallas_call x1, Pallas kernels, body(): pl.pallas_call(kernel, out_shape=(jax.ShapeDtypeStruct((3, TILES, 32, 128...  53.2 us
    pallas_call x1, Pallas kernels, body(): pl.pallas_call(finish, out_shape=(state, state, state, jax.ShapeDtypeStru...  2.25 us

profile of v1, /device:TPU:1, one launch (start us, length us, event | category | flops | bytes accessed | tf_op | source)
XLA Modules:
  0.0 56.1 jit_solution(5804274524983399981)
XLA Ops:
  0.6 53.2 %shard_map.93 = (f32[3,10,32,128]{3,2,1,0:T(8,128)}, bf16[8,4,40,128]{3,2,1,0:T(8,128)(2,1)}) custom-call(bf16[32,16,10,2,128]{4,3,2,1,0:T(2,128)(2,1)} %bitcast.30, f32[10,2,512]{2,1,0:T(2,128)} %bitcast.36, f32[16,10,2,128]{3,2,1,0:T(2,128)} %bitcast.33, f32[16,10,2,128]{3,2,1,0:T(2,128)} %bitcast.34, f32[16,10,2,128]{3,2,1,0:T(2,128)} %bitcast.35, ...), custom_call_target="tpu_custom_call" | custom-call | tf_op jit(solution)/shard_map/pallas_call | solution.py:377
  53.8 2.3 %shard_map.94 = (f32[16,10,2,128]{3,2,1,0:T(2,128)}, f32[16,10,2,128]{3,2,1,0:T(2,128)}, f32[16,10,2,128]{3,2,1,0:T(2,128)}, bf16[8,80,2,128]{3,2,1,0:T(2,128)(2,1)}) custom-call(f32[3,10,16,2,128]{4,3,2,1,0:T(2,128)} %bitcast.31, bf16[8,8,10,2,128]{4,3,2,1,0:T(2,128)(2,1)} %bitcast.32), custom_call_target="tpu_custom_call" | custom-call | tf_op jit(solution)/shard_map/pallas_call | solution.py:398

commit v2 on v0

v2 whole, which is shorter than its diff:
```python
import jax
import jax.numpy as jnp
from jax import lax
from jax.experimental import pallas as pl
from jax.experimental.layout import Layout, with_layout_constraint
from jax.experimental.pallas import tpu as pltpu
from jax.sharding import PartitionSpec as P

STEP = 100
ROWS = 16
TILES = 10
LINES = ROWS * TILES * 2
HALF = LINES // 2
SIDE = 4
CHIPS = SIDE * SIDE
DEPTH = 8
NDP = 32
KEYS = 64
MESH = pl.DeviceIdType.MESH
BF16 = jnp.bfloat16
F32 = jnp.float32
GROUPS = (0, 1)
CHUNKS = ((0, 10),)
OFFSETS = (2, 1, 3, 0)


def iota(shape, dim):
    return lax.broadcasted_iota(jnp.int32, shape, dim)


def scratch():
    made = {
        "scale": pltpu.VMEM((2, TILES, 2, 512), F32),
        "keys": pltpu.VMEM((2, CHIPS, 2, ROWS, KEYS), BF16),
        "spread": pltpu.VMEM((2, CHIPS, LINES, 128), F32),
        "state": pltpu.VMEM((3, LINES, 128), F32),
        "fresh": pltpu.VMEM((3, LINES, 128), F32),
        "rounded": pltpu.VMEM((LINES, 128), BF16),
        "owner": pltpu.VMEM((1, ROWS), jnp.int32),
        "load_sem": pltpu.SemaphoreType.DMA((2,)),
        "scale_sem": pltpu.SemaphoreType.DMA((4,)),
        "state_sem": pltpu.SemaphoreType.DMA((3,)),
        "fresh_sem": pltpu.SemaphoreType.DMA,
    }
    block = (HALF, 128)
    for g in GROUPS:
        made |= {
            f"mine{g}": pltpu.VMEM((SIDE, SIDE) + block, BF16),
            f"take{g}": pltpu.VMEM((SIDE, SIDE) + block, BF16),
            f"own{g}": pltpu.VMEM((SIDE,) + block, F32),
            f"first{g}": pltpu.VMEM((3, SIDE) + block, BF16),
            f"first_in{g}": pltpu.VMEM((3, SIDE) + block, BF16),
            f"second{g}": pltpu.VMEM((3,) + block, BF16),
            f"second_in{g}": pltpu.VMEM((3,) + block, BF16),
            f"total{g}": pltpu.VMEM(block, F32),
            f"pair_sem{g}": pltpu.SemaphoreType.DMA((2, 4)),
            f"first_sem{g}": pltpu.SemaphoreType.DMA((2, 3)),
            f"second_sem{g}": pltpu.SemaphoreType.DMA((2, 3)),
        }
    for h, (_, n) in enumerate(CHUNKS):
        made |= {
            f"select{h}": pltpu.VMEM((128 * n, LINES), BF16),
            f"slots{h}": pltpu.VMEM((NDP, 4 * n, 128), BF16),
            f"plane{h}": pltpu.VMEM((DEPTH, 4, 4 * n, 128), BF16),
            f"plane_sem{h}": pltpu.SemaphoreType.DMA((2, NDP)),
            f"deep_sem{h}": pltpu.SemaphoreType.DMA((2, DEPTH)),
        }
    return made


NAMES = tuple(scratch())


def kernel(pay_in, scale_in, master_in, one_in, two_in, owner_in, *rest):
    fresh_out, next_out = rest[0], rest[1 : 1 + len(CHUNKS)]
    r = dict(zip(NAMES, rest[1 + len(CHUNKS) :]))
    dp, z = lax.axis_index("dp"), lax.axis_index("mp")
    c, y, x = dp % 2, dp // 2 % SIDE, dp // (2 * SIDE)
    centre = ((x, y), (y, x))

    def place(px, py, pc):
        return (px * SIDE + py) * 2 + pc

    def near(g, a):
        return (place(a, y, c), z) if g == 0 else (place(x, a, c), z)

    def remote(src, dst, sems, i, j, device):
        return pltpu.make_async_remote_copy(
            src, dst, sems.at[0, i], sems.at[1, j], device_id=device, device_id_type=MESH
        )

    sibling = (place(x, y, 1 - c), z)
    greeted = [sibling]
    greeted += [near(g, (centre[g][0] + i) % SIDE) for i in range(1, SIDE) for g in GROUPS]
    greeted += [(dp, (z + i) % DEPTH) for i in range(1, DEPTH)]
    barrier = pltpu.get_barrier_semaphore()
    for device in greeted:
        pl.semaphore_signal(barrier, inc=1, device_id=device, device_id_type=MESH)

    scale_load = pltpu.make_async_copy(scale_in, r["scale"].at[0], r["scale_sem"].at[0])
    scale_load.start()
    owner_load = pltpu.make_async_copy(owner_in, r["owner"], r["scale_sem"].at[1])
    owner_load.start()
    loads = [
        pltpu.make_async_copy(
            pay_in.at[:, :, c, pl.ds(HALF * g, HALF)], r[f"mine{g}"], r["load_sem"].at[g]
        )
        for g in GROUPS
    ]
    state_loads = [
        pltpu.make_async_copy(ref, r["state"].at[i], r["state_sem"].at[i])
        for i, ref in enumerate((master_in, one_in, two_in))
    ]
    for copy in loads + state_loads:
        copy.start()
    pl.semaphore_wait(barrier, len(greeted))

    scale_pair = pltpu.make_async_remote_copy(
        scale_in,
        r["scale"].at[1],
        r["scale_sem"].at[2],
        r["scale_sem"].at[3],
        device_id=sibling,
        device_id_type=MESH,
    )
    scale_pair.start()
    pair = {}
    for k in range(4):
        for g in GROUPS:
            a = (centre[g][0] + OFFSETS[k]) % SIDE
            lines = pl.ds(HALF * g, HALF)
            source = pay_in.at[a, :, 1 - c, lines] if g == 0 else pay_in.at[:, a, 1 - c, lines]
            target = r[f"take{g}"].at[a] if g == 0 else r[f"take{g}"].at[:, a]
            pair[g, k] = remote(source, target, r[f"pair_sem{g}"], k, k, sibling)
            pair[g, k].start()

    eye = (iota((128, 128), 0) == iota((128, 128), 1)).astype(BF16)
    repeat = (iota((2 * LINES, 2 * ROWS), 0) // (2 * TILES) == iota((2 * LINES, 2 * ROWS), 1)).astype(
        BF16
    )
    line = iota((2 * LINES, KEYS), 0) % (2 * TILES)
    match = iota((2 * LINES, KEYS), 1) % (2 * TILES) == line % 2 * TILES + line // 2
    ones = jnp.ones((KEYS, 128), BF16)

    def spread(core):
        for k in range(4):
            whole = [r["scale"][core, :, i, 128 * k : 128 * k + 128] for i in range(2)]
            parts = []
            for _ in range(3):
                part = [value.astype(BF16).astype(F32) for value in whole]
                whole = [value - close for value, close in zip(whole, part)]
                parts += part
            parts = jnp.concatenate(parts + [jnp.zeros((KEYS - 60, 128), F32)], axis=0)
            turned = lax.dot_general(
                eye, parts.astype(BF16), (((1,), (1,)), ((), ())), preferred_element_type=F32
            )
            r["keys"][core, 4 * k : 4 * k + 4] = turned.astype(BF16).reshape(4, 2, ROWS, KEYS)

        def widen(i, carry):
            keys = r["keys"][core, pl.ds(2 * i, 2), c].reshape(2 * ROWS, KEYS)
            many = jnp.dot(repeat, keys, preferred_element_type=F32)
            many = jnp.where(match, many, 0.0).astype(BF16)
            wide = jnp.dot(many, ones, preferred_element_type=F32)
            r["spread"][core, pl.ds(2 * i, 2)] = wide.reshape(2, LINES, 128)
            return carry

        lax.fori_loop(0, CHIPS // 2, widen, 0)

    scale_load.wait()
    spread(0)
    scale_pair.wait_recv()
    spread(1)
    for copy in loads:
        copy.wait()

    first = {}
    for k in range(4):
        for g in GROUPS:
            a = (centre[g][0] + OFFSETS[k]) % SIDE
            pair[g, k].wait_recv()

            def add(b, carry, g=g, k=k, a=a):
                i, j = (a, b) if g == 0 else (b, a)
                lines = slice(HALF * g, HALF * g + HALF)
                total = r[f"mine{g}"][i, j].astype(F32) * r["spread"][0, i * SIDE + j, lines]
                total += r[f"take{g}"][i, j].astype(F32) * r["spread"][1, i * SIDE + j, lines]
                if k < 3:
                    r[f"first{g}"][k, b] = total.astype(BF16)
                else:
                    r[f"own{g}"][b] = total
                return carry

            lax.fori_loop(0, SIDE, add, 0)
            if k < 3:
                first[g, k] = remote(
                    r[f"first{g}"].at[k],
                    r[f"first_in{g}"].at[k],
                    r[f"first_sem{g}"],
                    k,
                    k,
                    near(g, a),
                )
                first[g, k].start()

    owner_load.wait()
    targets = r["owner"][...].astype(F32)
    square = (ROWS, ROWS)
    diagonal = jnp.where(iota(square, 0) == iota(square, 1), jnp.broadcast_to(targets, square), 0.0)
    columns = jnp.dot(diagonal.astype(BF16), jnp.ones(square, BF16), preferred_element_type=F32)
    earlier = (columns == targets) & (iota(square, 0) < iota(square, 1))
    rank = jnp.sum(jnp.where(earlier, 1.0, 0.0), axis=0, keepdims=True)
    slot = jnp.broadcast_to(targets * 2.0 + rank, (8, ROWS)).astype(BF16)
    wide = (ROWS, LINES)
    stretch = (iota(wide, 1) // (2 * TILES) == iota(wide, 0)).astype(BF16)
    slot = jnp.dot(slot, stretch, preferred_element_type=F32)[0:1].astype(jnp.int32)
    line = iota((1, LINES), 1) % (2 * TILES)
    for h, (h0, n) in enumerate(CHUNKS):
        inside = (line >= 2 * h0) & (line < 2 * h0 + 2 * n)
        goal = jnp.where(inside, slot * (2 * n) + line - 2 * h0, -1)
        r[f"select{h}"][...] = (iota((128 * n, LINES), 0) == goal).astype(BF16)
    for copy in state_loads:
        copy.wait()

    second = {}
    for g in GROUPS:
        a, b0 = centre[g]
        for k in range(3):
            first[g, k].wait_recv()
        for k in range(4):
            b = (b0 + OFFSETS[k]) % SIDE
            total = r[f"own{g}"][b]
            for j in range(3):
                total += r[f"first_in{g}"][j, b].astype(F32)
            if k == 3:
                r[f"total{g}"][...] = total
                continue
            r[f"second{g}"][k] = total.astype(BF16)
            second[g, k] = remote(
                r[f"second{g}"].at[k],
                r[f"second_in{g}"].at[k],
                r[f"second_sem{g}"],
                k,
                k,
                near(1 - g, b),
            )
            second[g, k].start()

    fix_one = 1.0 - 0.9 ** (STEP + 1)
    fix_two = 1.0 - 0.95 ** (STEP + 1)
    for g in GROUPS:
        for k in range(3):
            second[g, k].wait_recv()
        lines = slice(HALF * g, HALF * g + HALF)
        grad = r[f"total{g}"][...]
        for j in range(3):
            grad += r[f"second_in{g}"][j].astype(F32)
        master, one, two = (r["state"][i, lines] for i in range(3))
        one = 0.9 * one + 0.1 * grad
        two = 0.95 * two + 0.05 * grad * grad
        direction = one / fix_one / (jnp.sqrt(two / fix_two) + 1e-08)
        master = master - 0.00015 * (direction + 0.1 * master)
        for i, value in enumerate((master, one, two)):
            r["fresh"][i, lines] = value
        r["rounded"][lines] = master.astype(BF16)
    for h, (_, n) in enumerate(CHUNKS):
        moved = jnp.dot(r[f"select{h}"][...], r["rounded"][...], preferred_element_type=F32)
        r[f"slots{h}"][...] = moved.reshape(NDP, 4 * n, 128).astype(BF16)

        def send(i, carry, h=h):
            d = (dp + i) % NDP
            remote(
                r[f"slots{h}"].at[d],
                r[f"plane{h}"].at[dp // 4, dp % 4],
                r[f"plane_sem{h}"],
                i,
                i,
                (d, z),
            ).start()
            return carry

        lax.fori_loop(1, NDP, send, 0)
        pltpu.make_async_copy(
            r[f"slots{h}"].at[dp], r[f"plane{h}"].at[dp // 4, dp % 4], r[f"plane_sem{h}"].at[0, 0]
        ).start()
    fresh_store = pltpu.make_async_copy(r["fresh"], fresh_out, r["fresh_sem"])
    fresh_store.start()

    deep = []
    for h, (_, n) in enumerate(CHUNKS):

        def land(i, carry, h=h):
            d = (dp + NDP - i) % NDP
            remote(
                r[f"slots{h}"].at[d],
                r[f"plane{h}"].at[d // 4, d % 4],
                r[f"plane_sem{h}"],
                i,
                i,
                (d, z),
            ).wait_recv()
            return carry

        lax.fori_loop(1, NDP, land, 0)
        pltpu.make_async_copy(
            r[f"slots{h}"].at[dp], r[f"plane{h}"].at[dp // 4, dp % 4], r[f"plane_sem{h}"].at[0, 0]
        ).wait()
        there = next_out[h].at[z]
        for i in (4, 3, 5, 2, 6, 1, 7):
            to = (z + i) % DEPTH
            copy = remote(r[f"plane{h}"].at[to], there, r[f"deep_sem{h}"], i, i, (dp, to))
            copy.start()
            deep.append(copy)
        copy = pltpu.make_async_copy(r[f"plane{h}"].at[z], there, r[f"deep_sem{h}"].at[0, 0])
        copy.start()
        deep.append(copy)
    for copy in [scale_pair] + list(pair.values()) + list(first.values()) + list(second.values()):
        copy.wait_send()
    for h in range(len(CHUNKS)):

        def sent(i, carry, h=h):
            d = (dp + i) % NDP
            remote(
                r[f"slots{h}"].at[d],
                r[f"plane{h}"].at[dp // 4, dp % 4],
                r[f"plane_sem{h}"],
                i,
                i,
                (d, z),
            ).wait_send()
            return carry

        lax.fori_loop(1, NDP, sent, 0)
    for copy in [fresh_store] + deep:
        copy.wait()


def finish(fresh, *rest):
    parts = len(CHUNKS)
    arrived, outs, rows_out = rest[:parts], rest[parts : parts + 3], rest[parts + 3]
    state, state_in_sem, state_sem, rows_in_sem, rows_sem = rest[parts + 4 : parts + 9]
    rows = rest[parts + 9 :]
    loads = [pltpu.make_async_copy(fresh, state, state_in_sem)]
    loads += [pltpu.make_async_copy(arrived[h], rows[h], rows_in_sem.at[h]) for h in range(parts)]
    for copy in loads:
        copy.start()
    copies = []

    def store(src, dst, sem):
        copies.append(pltpu.make_async_copy(src, dst, sem))
        copies[-1].start()

    loads[0].wait()
    for i in range(3):
        store(state.at[i], outs[i], state_sem.at[i])
    for h, (h0, n) in enumerate(CHUNKS):
        loads[1 + h].wait()
        for m in range(DEPTH):
            store(rows[h].at[m], rows_out.at[:, pl.ds(m * TILES + h0, n)], rows_sem.at[h, m])
    for copy in copies:
        copy.wait()


def body(payload, block_scale, master, moment_one, moment_two, owner):
    def plain(array):
        return with_layout_constraint(array, Layout(tuple(range(array.ndim))))

    def fold(array, shape):
        split = array.shape[:-1] + (array.shape[-1] // 128, 128)
        return plain(jnp.swapaxes(array.reshape(split), -3, -2)).reshape(shape)

    def unfold(array):
        array = jnp.swapaxes(array, -3, -2)
        return array.reshape(array.shape[:-2] + (-1,))

    anywhere = pl.BlockSpec(memory_space=pl.ANY)
    fresh, *arrived = pl.pallas_call(
        kernel,
        out_shape=(
            jax.ShapeDtypeStruct((3, LINES, 128), F32),
            *(jax.ShapeDtypeStruct((DEPTH, 4, 4 * n, 128), BF16) for _, n in CHUNKS),
        ),
        in_specs=[anywhere] * 6,
        out_specs=(anywhere,) * (1 + len(CHUNKS)),
        scratch_shapes=list(scratch().values()),
        compiler_params=pltpu.CompilerParams(
            collective_id=0, has_side_effects=True, vmem_limit_bytes=60 * 2**20
        ),
    )(
        fold(payload[0], (SIDE, SIDE, 2, LINES, 128)),
        jnp.transpose(block_scale[0], (2, 1, 0)),
        fold(master, (LINES, 128)),
        fold(moment_one, (LINES, 128)),
        fold(moment_two, (LINES, 128)),
        owner.T,
    )
    state = jax.ShapeDtypeStruct((ROWS, TILES, 2, 128), F32)
    results = pl.pallas_call(
        finish,
        out_shape=(state, state, state, jax.ShapeDtypeStruct((8, DEPTH * TILES, 2, 128), BF16)),
        in_specs=[anywhere] * (1 + len(CHUNKS)),
        out_specs=(anywhere,) * 4,
        scratch_shapes=[
            pltpu.VMEM((3, ROWS, TILES, 2, 128), F32),
            pltpu.SemaphoreType.DMA,
            pltpu.SemaphoreType.DMA((3,)),
            pltpu.SemaphoreType.DMA((len(CHUNKS),)),
            pltpu.SemaphoreType.DMA((len(CHUNKS), DEPTH)),
            *(pltpu.VMEM((DEPTH, 8, n, 2, 128), BF16) for _, n in CHUNKS),
        ],
    )(
        fresh.reshape(3, ROWS, TILES, 2, 128),
        *(part.reshape(DEPTH, 8, n, 2, 128) for part, (_, n) in zip(arrived, CHUNKS)),
    )
    return tuple(unfold(result) for result in results)


def solution(mesh):
    return jax.shard_map(
        body,
        mesh=mesh,
        in_specs=(
            P("dp", None, None, "mp"),
            P("dp", None, None, "mp"),
            P("dp", None, "mp"),
            P("dp", None, "mp"),
            P("dp", None, "mp"),
            P("dp", None),
        ),
        out_specs=(
            P("dp", None, "mp"),
            P("dp", None, "mp"),
            P("dp", None, "mp"),
            P(("dp", "mp"), None, None),
        ),
        check_vma=False,
    )
```

time: 191 us -> 49.4 us (0.26)
  waiting for transfers between devices: 120 us -> 0 us
  Pallas kernels: 0 us -> 48.6 us
  blocking collectives: 35.8 us -> 0 us
  local copies, waits for them, and re-layouts: 14.4 us -> 0 us
  between operations: 14.8 us -> 0.64 us
  other arithmetic: 4.66 us -> 0 us
    unnamed x2 -> x0, waiting for transfers between devices: 120 us -> none
    pallas_call x0 -> x2, Pallas kernels: none -> 48.6 us  [the longest x1 46.6 us: body(): pl.pallas_call(kernel, out_shape=(jax.ShapeDtypeStruct((3, LINES, 128), F...]
    all_to_all x2 -> x0, blocking collectives: 35.8 us -> none  [the longest x1 20.3 us: body(): lax.all_to_all(lax.all_to_all(outgoing, 'dp', split_axis=0, concat_axis=0...]
    unnamed x15 -> x0, local copies, waits for them, and re-layouts: 8.62 us -> none
    convert_element_type x1 -> x0, local copies, waits for them, and re-layouts: 4.83 us -> none  [body(): dequantize(values, scales).astype(jnp.bfloat16)]
    convert_element_type x2 -> x0, other arithmetic: 4.47 us -> none  [the longest x1 2.25 us: body(): dequantize(values, scales).astype(jnp.bfloat16)]
  transfers between devices with their start and end apart: 1 -> 0, of which waited for: 1 -> 0; matrix products, arithmetic and copies ran while one was open for 0% -> 0% of each run, Pallas kernels for 0% -> 0%
where the time goes in v2:
time: 49.4 us; the launch traced here: 49.3 us
  Pallas kernels  48.6 us (98%)
  between operations  0.64 us (1%)
    pallas_call x1, Pallas kernels, body(): pl.pallas_call(kernel, out_shape=(jax.ShapeDtypeStruct((3, LINES, 128), F...  46.6 us
    pallas_call x1, Pallas kernels, body(): pl.pallas_call(finish, out_shape=(state, state, state, jax.ShapeDtypeStru...  2.02 us

profile of v2, /device:TPU:1, one launch (start us, length us, event | category | flops | bytes accessed | tf_op | source)
XLA Modules:
  0.0 49.3 jit_solution(13646315246000842902)
XLA Ops:
  0.6 46.6 %shard_map.93 = (f32[3,320,128]{2,1,0:T(8,128)}, bf16[8,4,40,128]{3,2,1,0:T(8,128)(2,1)}) custom-call(bf16[4,4,2,320,128]{4,3,2,1,0:T(8,128)(2,1)} %bitcast.38, f32[10,2,512]{2,1,0:T(2,128)} %bitcast.44, f32[320,128]{1,0:T(8,128)} %bitcast.41, f32[320,128]{1,0:T(8,128)} %bitcast.42, f32[320,128]{1,0:T(8,128)} %bitcast.43, s32[1,16]{1,0:T(1,128)} %bitcast.45), custom_call_target="tpu_custom_call" | custom-call | tf_op jit(solution)/shard_map/pallas_call | solution.py:376
  47.3 2.0 %shard_map.94 = (f32[16,10,2,128]{3,2,1,0:T(2,128)}, f32[16,10,2,128]{3,2,1,0:T(2,128)}, f32[16,10,2,128]{3,2,1,0:T(2,128)}, bf16[8,80,2,128]{3,2,1,0:T(2,128)(2,1)}) custom-call(f32[3,16,10,2,128]{4,3,2,1,0:T(2,128)} %bitcast.39, bf16[8,8,10,2,128]{4,3,2,1,0:T(2,128)(2,1)} %bitcast.40), custom_call_target="tpu_custom_call" | custom-call | tf_op jit(solution)/shard_map/pallas_call | solution.py:397

commit v3 on v2

v3 whole, which is shorter than its diff:
```python
from types import SimpleNamespace

import jax
import jax.numpy as jnp
from jax import lax
from jax.experimental import pallas as pl
from jax.experimental.layout import Layout, with_layout_constraint
from jax.experimental.pallas import tpu as pltpu
from jax.sharding import PartitionSpec as P

STEP = 100
ROWS = 16
TILES = 10
LINES = ROWS * TILES * 2
HALF = LINES // 2
SIDE = 4
DEPTH = 8
NDP = 32
KEYS = 64
MESH = pl.DeviceIdType.MESH
BF16 = jnp.bfloat16
F32 = jnp.float32
GROUPS = (0, 1)
CHUNKS = ((0, 10),)
OFFSETS = (2, 1, 3, 0)


def iota(shape, dim):
    return lax.broadcasted_iota(jnp.int32, shape, dim)


def scratch():
    block = (HALF, 128)
    dma = pltpu.SemaphoreType.DMA

    def both(*args):
        return tuple(pltpu.VMEM(*args) for _ in GROUPS)

    return dict(
        scale=pltpu.VMEM((2, TILES, 2, 512), F32),
        keys=pltpu.VMEM((SIDE, SIDE, 2, ROWS, 2 * KEYS), F32),
        state=pltpu.VMEM((3, LINES, 128), F32),
        fresh=pltpu.VMEM((3, LINES, 128), F32),
        rounded=pltpu.VMEM((LINES, 128), BF16),
        owner=pltpu.VMEM((1, ROWS), jnp.int32),
        load_sem=dma((2, 4)),
        scale_sem=dma((4,)),
        state_sem=dma((3,)),
        fresh_sem=dma,
        known=pltpu.SemaphoreType.REGULAR((2, 3)),
        mine=both((4, SIDE) + block, BF16),
        take=both((4, SIDE) + block, BF16),
        own=both((SIDE,) + block, F32),
        first=both((3, SIDE) + block, BF16),
        relay_in=both((2, 2) + block, BF16),
        hold=both((2, 2) + block, F32),
        first_in=both((2, SIDE) + block, BF16),
        second=both((3,) + block, BF16),
        second_in=both((3,) + block, BF16),
        total=both(block, F32),
        pair_sem=tuple(dma((2, 4)) for _ in GROUPS),
        first_sem=tuple(dma((2, 6)) for _ in GROUPS),
        second_sem=tuple(dma((2, 3)) for _ in GROUPS),
        select=tuple(pltpu.VMEM((128 * n, LINES), BF16) for _, n in CHUNKS),
        slots=tuple(pltpu.VMEM((NDP, 4 * n, 128), BF16) for _, n in CHUNKS),
        plane=tuple(pltpu.VMEM((DEPTH, 4, 4 * n, 128), BF16) for _, n in CHUNKS),
        plane_sem=tuple(dma((2, NDP)) for _ in CHUNKS),
        deep_sem=tuple(dma((2, DEPTH)) for _ in CHUNKS),
    )


SCRATCH, TREE = jax.tree.flatten(scratch(), is_leaf=lambda leaf: not isinstance(leaf, (dict, tuple)))


def kernel(pay_in, scale_in, master_in, one_in, two_in, owner_in, *rest):
    fresh_out, next_out = rest[0], rest[1 : 1 + len(CHUNKS)]
    r = SimpleNamespace(**jax.tree.unflatten(TREE, rest[1 + len(CHUNKS) :]))
    dp, z = lax.axis_index("dp"), lax.axis_index("mp")
    c, y, x = dp % 2, dp // 2 % SIDE, dp // (2 * SIDE)
    centre = ((x, y), (y, x))

    def place(px, py, pc):
        return (px * SIDE + py) * 2 + pc

    def near(g, a):
        return (place(a, y, c), z) if g == 0 else (place(x, a, c), z)

    def remote(src, dst, sems, i, j, device):
        return pltpu.make_async_remote_copy(
            src, dst, sems.at[0, i], sems.at[1, j], device_id=device, device_id_type=MESH
        )

    sibling = (place(x, y, 1 - c), z)
    greeted = [sibling]
    greeted += [near(g, (centre[g][0] + i) % SIDE) for i in range(1, SIDE) for g in GROUPS]
    below, above = (dp, (z + DEPTH - 1) % DEPTH), (dp, (z + 1) % DEPTH)
    greeted += [below, above]
    barrier = pltpu.get_barrier_semaphore()
    for device in greeted:
        pl.semaphore_signal(barrier, inc=1, device_id=device, device_id_type=MESH)

    scale_load = pltpu.make_async_copy(scale_in, r.scale.at[0], r.scale_sem.at[0])
    scale_load.start()
    owner_load = pltpu.make_async_copy(owner_in, r.owner, r.scale_sem.at[1])
    owner_load.start()

    def part(g, k, core):
        a = (centre[g][0] + OFFSETS[k]) % SIDE
        lines = pl.ds(HALF * g, HALF)
        return pay_in.at[a, :, core, lines] if g == 0 else pay_in.at[:, a, core, lines]

    loads = {
        (g, k): pltpu.make_async_copy(part(g, k, c), r.mine[g].at[k], r.load_sem.at[g, k])
        for k in range(4)
        for g in GROUPS
    }
    state_loads = [
        pltpu.make_async_copy(ref, r.state.at[i], r.state_sem.at[i])
        for i, ref in enumerate((master_in, one_in, two_in))
    ]
    for copy in list(loads.values()) + state_loads:
        copy.start()
    pl.semaphore_wait(barrier, len(greeted))

    scale_pair = pltpu.make_async_remote_copy(
        scale_in,
        r.scale.at[1],
        r.scale_sem.at[2],
        r.scale_sem.at[3],
        device_id=sibling,
        device_id_type=MESH,
    )
    scale_pair.start()
    pair = {}
    for k in range(4):
        for g in GROUPS:
            pair[g, k] = remote(
                part(g, k, 1 - c), r.take[g].at[k], r.pair_sem[g], k, k, sibling
            )
            pair[g, k].start()

    def tell(step):
        for way, device in ((0, above), (1, below)):
            if (way, step) != (0, 2):
                pl.semaphore_signal(
                    r.known.at[way, step], inc=1, device_id=device, device_id_type=MESH
                )

    def learn(step):
        for way in range(2):
            if (way, step) != (0, 2):
                pl.semaphore_wait(r.known.at[way, step], 1)

    tell(0)

    scale_load.wait()
    scale_pair.wait_recv()
    eye = (iota((128, 128), 0) == iota((128, 128), 1)).astype(BF16)
    for k in range(4):
        parts = []
        for core in range(2):
            whole = [r.scale[core, :, i, 128 * k : 128 * k + 128] for i in range(2)]
            for _ in range(3):
                near_by = [value.astype(BF16).astype(F32) for value in whole]
                whole = [value - close for value, close in zip(whole, near_by)]
                parts += near_by
            parts.append(jnp.zeros((KEYS - 60, 128), F32))
        turned = lax.dot_general(
            eye,
            jnp.concatenate(parts, axis=0).astype(BF16),
            (((1,), (1,)), ((), ())),
            preferred_element_type=F32,
        )
        r.keys[k] = turned.reshape(4, 2, ROWS, 2 * KEYS)

    unit = SIDE * HALF
    repeat = (iota((unit, 32), 0) // (2 * TILES) == iota((unit, 32), 1)).astype(BF16)
    line = iota((unit, 2 * KEYS), 0) % (2 * TILES)
    match = iota((unit, 2 * KEYS), 1) % KEYS % (2 * TILES) == line % 2 * TILES + line // 2
    ones = (iota((2 * KEYS, 256), 0) // KEYS == iota((2 * KEYS, 256), 1) // 128).astype(BF16)

    def terms(g, k):
        a = (centre[g][0] + OFFSETS[k]) % SIDE
        rows = slice(8 * g, 8 * g + 8)
        keys = r.keys[a, :, c, rows] if g == 0 else r.keys[:, a, c, rows]
        many = jnp.dot(repeat, keys.reshape(32, 2 * KEYS).astype(BF16), preferred_element_type=F32)
        many = jnp.where(match, many, 0.0).astype(BF16)
        scales = jnp.dot(many, ones, preferred_element_type=F32)
        loads[g, k].wait()
        pair[g, k].wait_recv()
        total = r.mine[g][k].astype(F32).reshape(unit, 128) * scales[:, :128]
        total += r.take[g][k].astype(F32).reshape(unit, 128) * scales[:, 128:]
        return total.reshape(SIDE, HALF, 128)

    first = {}
    lower, upper = slice(0, 2), slice(2, 4)

    def pass_on(g, number, source, target, step):
        first[g, number] = remote(
            source,
            target,
            r.first_sem[g],
            number,
            number,
            near(g, (centre[g][0] + step) % SIDE),
        )
        first[g, number].start()

    for g in GROUPS:
        r.first[g][0] = terms(g, 0).astype(BF16)
        sent_ref, relay = r.first[g].at[0], r.relay_in[g]
        pass_on(g, 0, sent_ref.at[pl.ds(0, 2)], relay.at[0], 1)
        pass_on(g, 1, sent_ref.at[pl.ds(2, 2)], relay.at[1], 3)
    for side, (k, step, now, later, start) in enumerate(
        ((1, 1, upper, lower, 2), (2, 3, lower, upper, 0))
    ):
        for g in GROUPS:
            total = terms(g, k)
            r.first[g][k, now] = total[now].astype(BF16)
            pass_on(
                g,
                2 + 2 * side,
                r.first[g].at[k, pl.ds(start, 2)],
                r.first_in[g].at[side, pl.ds(start, 2)],
                step,
            )
            r.hold[g][side] = total[later]
    for side, (k, step, later, start) in enumerate(((1, 1, lower, 0), (2, 3, upper, 2))):
        for g in GROUPS:
            first[g, side].wait_recv()
            r.first[g][k, later] = (
                r.hold[g][side] + r.relay_in[g][side].astype(F32)
            ).astype(BF16)
            pass_on(
                g,
                3 + 2 * side,
                r.first[g].at[k, pl.ds(start, 2)],
                r.first_in[g].at[side, pl.ds(start, 2)],
                step,
            )
    for g in GROUPS:
        r.own[g][...] = terms(g, 3)
    learn(0)
    tell(1)

    owner_load.wait()
    targets = r.owner[...].astype(F32)
    square = (ROWS, ROWS)
    diagonal = jnp.where(iota(square, 0) == iota(square, 1), jnp.broadcast_to(targets, square), 0.0)
    columns = jnp.dot(diagonal.astype(BF16), jnp.ones(square, BF16), preferred_element_type=F32)
    earlier = (columns == targets) & (iota(square, 0) < iota(square, 1))
    rank = jnp.sum(jnp.where(earlier, 1.0, 0.0), axis=0, keepdims=True)
    slot = jnp.broadcast_to(targets * 2.0 + rank, (8, ROWS)).astype(BF16)
    wide = (ROWS, LINES)
    stretch = (iota(wide, 1) // (2 * TILES) == iota(wide, 0)).astype(BF16)
    slot = jnp.dot(slot, stretch, preferred_element_type=F32)[0:1].astype(jnp.int32)
    line = iota((1, LINES), 1) % (2 * TILES)
    for h, (h0, n) in enumerate(CHUNKS):
        inside = (line >= 2 * h0) & (line < 2 * h0 + 2 * n)
        goal = jnp.where(inside, slot * (2 * n) + line - 2 * h0, -1)
        r.select[h][...] = (iota((128 * n, LINES), 0) == goal).astype(BF16)
    for copy in state_loads:
        copy.wait()

    learn(1)
    tell(2)

    second = {}
    for g in GROUPS:
        b0 = centre[g][1]
        for number in range(2, 6):
            first[g, number].wait_recv()
        for k in range(4):
            b = (b0 + OFFSETS[k]) % SIDE
            total = r.own[g][b]
            for j in range(2):
                total += r.first_in[g][j, b].astype(F32)
            if k == 3:
                r.total[g][...] = total
                continue
            r.second[g][k] = total.astype(BF16)
            second[g, k] = remote(
                r.second[g].at[k],
                r.second_in[g].at[k],
                r.second_sem[g],
                k,
                k,
                near(1 - g, b),
            )
            second[g, k].start()

    fix_one = 1.0 - 0.9 ** (STEP + 1)
    fix_two = 1.0 - 0.95 ** (STEP + 1)
    for g in GROUPS:
        for k in range(3):
            second[g, k].wait_recv()
        lines = slice(HALF * g, HALF * g + HALF)
        grad = r.total[g][...]
        for j in range(3):
            grad += r.second_in[g][j].astype(F32)
        master, one, two = (r.state[i, lines] for i in range(3))
        one = 0.9 * one + 0.1 * grad
        two = 0.95 * two + 0.05 * grad * grad
        direction = one / fix_one / (jnp.sqrt(two / fix_two) + 1e-08)
        master = master - 0.00015 * (direction + 0.1 * master)
        for i, value in enumerate((master, one, two)):
            r.fresh[i, lines] = value
        r.rounded[lines] = master.astype(BF16)
    for h, (_, n) in enumerate(CHUNKS):
        moved = jnp.dot(r.select[h][...], r.rounded[...], preferred_element_type=F32)
        r.slots[h][...] = moved.reshape(NDP, 4 * n, 128).astype(BF16)

        def send(i, carry, h=h):
            d = (dp + i) % NDP
            remote(
                r.slots[h].at[d],
                r.plane[h].at[dp // 4, dp % 4],
                r.plane_sem[h],
                i,
                i,
                (d, z),
            ).start()
            return carry

        lax.fori_loop(1, NDP, send, 0)
        pltpu.make_async_copy(
            r.slots[h].at[dp], r.plane[h].at[dp // 4, dp % 4], r.plane_sem[h].at[0, 0]
        ).start()
    fresh_store = pltpu.make_async_copy(r.fresh, fresh_out, r.fresh_sem)
    fresh_store.start()

    learn(2)
    deep = []
    for h, (_, n) in enumerate(CHUNKS):

        def land(i, carry, h=h):
            d = (dp + NDP - i) % NDP
            remote(
                r.slots[h].at[d],
                r.plane[h].at[d // 4, d % 4],
                r.plane_sem[h],
                i,
                i,
                (d, z),
            ).wait_recv()
            return carry

        lax.fori_loop(1, NDP, land, 0)
        pltpu.make_async_copy(
            r.slots[h].at[dp], r.plane[h].at[dp // 4, dp % 4], r.plane_sem[h].at[0, 0]
        ).wait()
        there = next_out[h].at[z]
        for i in (4, 3, 5, 2, 6, 1, 7):
            to = (z + i) % DEPTH
            copy = remote(r.plane[h].at[to], there, r.deep_sem[h], i, i, (dp, to))
            copy.start()
            deep.append(copy)
        copy = pltpu.make_async_copy(r.plane[h].at[z], there, r.deep_sem[h].at[0, 0])
        copy.start()
        deep.append(copy)
    for copy in [scale_pair] + list(pair.values()) + list(first.values()) + list(second.values()):
        copy.wait_send()
    for h in range(len(CHUNKS)):

        def sent(i, carry, h=h):
            d = (dp + i) % NDP
            remote(
                r.slots[h].at[d],
                r.plane[h].at[dp // 4, dp % 4],
                r.plane_sem[h],
                i,
                i,
                (d, z),
            ).wait_send()
            return carry

        lax.fori_loop(1, NDP, sent, 0)
    for copy in [fresh_store] + deep:
        copy.wait()


def finish(fresh, *rest):
    parts = len(CHUNKS)
    arrived, outs, rows_out = rest[:parts], rest[parts : parts + 3], rest[parts + 3]
    state, state_in_sem, state_sem, rows_in_sem, rows_sem = rest[parts + 4 : parts + 9]
    rows = rest[parts + 9 :]
    loads = [pltpu.make_async_copy(fresh, state, state_in_sem)]
    loads += [pltpu.make_async_copy(arrived[h], rows[h], rows_in_sem.at[h]) for h in range(parts)]
    for copy in loads:
        copy.start()
    copies = []

    def store(src, dst, sem):
        copies.append(pltpu.make_async_copy(src, dst, sem))
        copies[-1].start()

    loads[0].wait()
    for i in range(3):
        store(state.at[i], outs[i], state_sem.at[i])
    for h, (h0, n) in enumerate(CHUNKS):
        loads[1 + h].wait()
        for m in range(DEPTH):
            store(rows[h].at[m], rows_out.at[:, pl.ds(m * TILES + h0, n)], rows_sem.at[h, m])
    for copy in copies:
        copy.wait()


def body(payload, block_scale, master, moment_one, moment_two, owner):
    def plain(array):
        return with_layout_constraint(array, Layout(tuple(range(array.ndim))))

    def fold(array, shape):
        split = array.shape[:-1] + (array.shape[-1] // 128, 128)
        return plain(jnp.swapaxes(array.reshape(split), -3, -2)).reshape(shape)

    def unfold(array):
        array = jnp.swapaxes(array, -3, -2)
        return array.reshape(array.shape[:-2] + (-1,))

    anywhere = pl.BlockSpec(memory_space=pl.ANY)
    fresh, *arrived = pl.pallas_call(
        kernel,
        out_shape=(
            jax.ShapeDtypeStruct((3, LINES, 128), F32),
            *(jax.ShapeDtypeStruct((DEPTH, 4, 4 * n, 128), BF16) for _, n in CHUNKS),
        ),
        in_specs=[anywhere] * 6,
        out_specs=(anywhere,) * (1 + len(CHUNKS)),
        scratch_shapes=SCRATCH,
        compiler_params=pltpu.CompilerParams(
            collective_id=0, has_side_effects=True, vmem_limit_bytes=60 * 2**20
        ),
    )(
        fold(payload[0], (SIDE, SIDE, 2, LINES, 128)),
        jnp.transpose(block_scale[0], (2, 1, 0)),
        fold(master, (LINES, 128)),
        fold(moment_one, (LINES, 128)),
        fold(moment_two, (LINES, 128)),
        owner.T,
    )
    state = jax.ShapeDtypeStruct((ROWS, TILES, 2, 128), F32)
    results = pl.pallas_call(
        finish,
        out_shape=(state, state, state, jax.ShapeDtypeStruct((8, DEPTH * TILES, 2, 128), BF16)),
        in_specs=[anywhere] * (1 + len(CHUNKS)),
        out_specs=(anywhere,) * 4,
        scratch_shapes=[
            pltpu.VMEM((3, ROWS, TILES, 2, 128), F32),
            pltpu.SemaphoreType.DMA,
            pltpu.SemaphoreType.DMA((3,)),
            pltpu.SemaphoreType.DMA((len(CHUNKS),)),
            pltpu.SemaphoreType.DMA((len(CHUNKS), DEPTH)),
            *(pltpu.VMEM((DEPTH, 8, n, 2, 128), BF16) for _, n in CHUNKS),
        ],
    )(
        fresh.reshape(3, ROWS, TILES, 2, 128),
        *(part.reshape(DEPTH, 8, n, 2, 128) for part, (_, n) in zip(arrived, CHUNKS)),
    )
    return tuple(unfold(result) for result in results)


def solution(mesh):
    return jax.shard_map(
        body,
        mesh=mesh,
        in_specs=(
            P("dp", None, None, "mp"),
            P("dp", None, None, "mp"),
            P("dp", None, "mp"),
            P("dp", None, "mp"),
            P("dp", None, "mp"),
            P("dp", None),
        ),
        out_specs=(
            P("dp", None, "mp"),
            P("dp", None, "mp"),
            P("dp", None, "mp"),
            P(("dp", "mp"), None, None),
        ),
        check_vma=False,
    )
```

time: 49.4 us -> 45 us (0.911)
  Pallas kernels: 48.6 us -> 44.3 us
    pallas_call x1, Pallas kernels: 46.6 us -> 42.3 us  [body(): pl.pallas_call(kernel, out_shape=(jax.ShapeDtypeStruct((3, LINES, 128), F...]
where the time goes in v3:
time: 45 us; the launch traced here: 44.9 us
  Pallas kernels  44.3 us (98%)
  between operations  0.64 us (1%)
    pallas_call x1, Pallas kernels, body(): pl.pallas_call(kernel, out_shape=(jax.ShapeDtypeStruct((3, LINES, 128), F...  42.3 us
    pallas_call x1, Pallas kernels, body(): pl.pallas_call(finish, out_shape=(state, state, state, jax.ShapeDtypeStru...  2.02 us

profile of v3, /device:TPU:1, one launch (start us, length us, event | category | flops | bytes accessed | tf_op | source)
XLA Modules:
  0.0 44.9 jit_solution(2037377342845121430)
XLA Ops:
  0.6 42.3 %shard_map.93 = (f32[3,320,128]{2,1,0:T(8,128)}, bf16[8,4,40,128]{3,2,1,0:T(8,128)(2,1)}) custom-call(bf16[4,4,2,320,128]{4,3,2,1,0:T(8,128)(2,1)} %bitcast.38, f32[10,2,512]{2,1,0:T(2,128)} %bitcast.44, f32[320,128]{1,0:T(8,128)} %bitcast.41, f32[320,128]{1,0:T(8,128)} %bitcast.42, f32[320,128]{1,0:T(8,128)} %bitcast.43, s32[1,16]{1,0:T(1,128)} %bitcast.45), custom_call_target="tpu_custom_call" | custom-call | tf_op jit(solution)/shard_map/pallas_call | solution.py:421
  42.9 2.0 %shard_map.94 = (f32[16,10,2,128]{3,2,1,0:T(2,128)}, f32[16,10,2,128]{3,2,1,0:T(2,128)}, f32[16,10,2,128]{3,2,1,0:T(2,128)}, bf16[8,80,2,128]{3,2,1,0:T(2,128)(2,1)}) custom-call(f32[3,16,10,2,128]{4,3,2,1,0:T(2,128)} %bitcast.39, bf16[8,8,10,2,128]{4,3,2,1,0:T(2,128)(2,1)} %bitcast.40), custom_call_target="tpu_custom_call" | custom-call | tf_op jit(solution)/shard_map/pallas_call | solution.py:442

commit v4 on v3

--- a/solution.py
+++ b/solution.py
@@ -23,6 +23,10 @@
 GROUPS = (0, 1)
 CHUNKS = ((0, 10),)
 OFFSETS = (2, 1, 3, 0)
+AWAY = sorted(
+    ((i, j, core) for i in range(SIDE) for j in range(SIDE) for core in range(2) if (i, j, core) != (0, 0, 0)),
+    key=lambda step: -min(step[0], SIDE - step[0]) - min(step[1], SIDE - step[1]),
+)
 
 
 def iota(shape, dim):
@@ -137,7 +141,8 @@
             pair[g, k] = remote(
                 part(g, k, 1 - c), r.take[g].at[k], r.pair_sem[g], k, k, sibling
             )
-            pair[g, k].start()
+    for g in GROUPS:
+        pair[g, 0].start()
 
     def tell(step):
         for way, device in ((0, above), (1, below)):
@@ -155,6 +160,9 @@
 
     scale_load.wait()
     scale_pair.wait_recv()
+    for k in range(1, 4):
+        for g in GROUPS:
+            pair[g, k].start()
     eye = (iota((128, 128), 0) == iota((128, 128), 1)).astype(BF16)
     for k in range(4):
         parts = []
@@ -306,75 +314,58 @@
         for i, value in enumerate((master, one, two)):
             r.fresh[i, lines] = value
         r.rounded[lines] = master.astype(BF16)
+    spread = []
     for h, (_, n) in enumerate(CHUNKS):
         moved = jnp.dot(r.select[h][...], r.rounded[...], preferred_element_type=F32)
         r.slots[h][...] = moved.reshape(NDP, 4 * n, 128).astype(BF16)
 
-        def send(i, carry, h=h):
-            d = (dp + i) % NDP
-            remote(
+        for i, j, core in AWAY:
+            d = place((x + i) % SIDE, (y + j) % SIDE, (c + core) % 2)
+            copy = remote(
                 r.slots[h].at[d],
                 r.plane[h].at[dp // 4, dp % 4],
                 r.plane_sem[h],
-                i,
-                i,
+                place(i, j, core),
+                place(i, j, core),
                 (d, z),
-            ).start()
-            return carry
-
-        lax.fori_loop(1, NDP, send, 0)
+            )
+            copy.start()
+            spread.append(copy)
         pltpu.make_async_copy(
-            r.slots[h].at[dp], r.plane[h].at[dp // 4, dp % 4], r.plane_sem[h].at[0, 0]
+            r.slots[h].at[dp], r.plane[h].at[dp // 4, dp % 4], r.plane_sem[h].at[1, 0]
         ).start()
     fresh_store = pltpu.make_async_copy(r.fresh, fresh_out, r.fresh_sem)
     fresh_store.start()
 
     learn(2)
     deep = []
+
+    def arrive(h, to):
+        for i in range(4):
+            source = 4 * to + i
+            away = place(
+                (x + SIDE - source // 8) % SIDE, (y + SIDE - source // 2 % SIDE) % SIDE, (c + source) % 2
+            )
+            slots = r.plane[h].at[to, i]
+            pltpu.make_async_copy(slots, slots, r.plane_sem[h].at[1, away]).wait()
+
     for h, (_, n) in enumerate(CHUNKS):
 
-        def land(i, carry, h=h):
-            d = (dp + NDP - i) % NDP
-            remote(
-                r.slots[h].at[d],
-                r.plane[h].at[d // 4, d % 4],
-                r.plane_sem[h],
-                i,
-                i,
-                (d, z),
-            ).wait_recv()
-            return carry
-
-        lax.fori_loop(1, NDP, land, 0)
-        pltpu.make_async_copy(
-            r.slots[h].at[dp], r.plane[h].at[dp // 4, dp % 4], r.plane_sem[h].at[0, 0]
-        ).wait()
         there = next_out[h].at[z]
         for i in (4, 3, 5, 2, 6, 1, 7):
             to = (z + i) % DEPTH
+            arrive(h, to)
             copy = remote(r.plane[h].at[to], there, r.deep_sem[h], i, i, (dp, to))
             copy.start()
             deep.append(copy)
+        arrive(h, z)
         copy = pltpu.make_async_copy(r.plane[h].at[z], there, r.deep_sem[h].at[0, 0])
         copy.start()
         deep.append(copy)
     for copy in [scale_pair] + list(pair.values()) + list(first.values()) + list(second.values()):
         copy.wait_send()
-    for h in range(len(CHUNKS)):
-
-        def sent(i, carry, h=h):
-            d = (dp + i) % NDP
-            remote(
-                r.slots[h].at[d],
-                r.plane[h].at[dp // 4, dp % 4],
-                r.plane_sem[h],
-                i,
-                i,
-                (d, z),
-            ).wait_send()
-            return carry
-
-        lax.fori_loop(1, NDP, sent, 0)
+    for copy in spread:
+        copy.wait_send()
     for copy in [fresh_store] + deep:
         copy.wait()
 
@@ -382,25 +373,17 @@
 def finish(fresh, *rest):
     parts = len(CHUNKS)
     arrived, outs, rows_out = rest[:parts], rest[parts : parts + 3], rest[parts + 3]
-    state, state_in_sem, state_sem, rows_in_sem, rows_sem = rest[parts + 4 : parts + 9]
-    rows = rest[parts + 9 :]
-    loads = [pltpu.make_async_copy(fresh, state, state_in_sem)]
-    loads += [pltpu.make_async_copy(arrived[h], rows[h], rows_in_sem.at[h]) for h in range(parts)]
-    for copy in loads:
+    state_sem, rows_sem = rest[parts + 4 :]
+    copies = [
+        pltpu.make_async_copy(
+            arrived[h].at[m], rows_out.at[:, pl.ds(m * TILES + h0, n)], rows_sem.at[h, m]
+        )
+        for h, (h0, n) in enumerate(CHUNKS)
+        for m in range(DEPTH)
+    ]
+    copies += [pltpu.make_async_copy(fresh.at[i], outs[i], state_sem.at[i]) for i in range(3)]
+    for copy in copies:
         copy.start()
-    copies = []
-
-    def store(src, dst, sem):
-        copies.append(pltpu.make_async_copy(src, dst, sem))
-        copies[-1].start()
-
-    loads[0].wait()
-    for i in range(3):
-        store(state.at[i], outs[i], state_sem.at[i])
-    for h, (h0, n) in enumerate(CHUNKS):
-        loads[1 + h].wait()
-        for m in range(DEPTH):
-            store(rows[h].at[m], rows_out.at[:, pl.ds(m * TILES + h0, n)], rows_sem.at[h, m])
     for copy in copies:
         copy.wait()
 
@@ -428,15 +411,17 @@
         out_specs=(anywhere,) * (1 + len(CHUNKS)),
         scratch_shapes=SCRATCH,
         compiler_params=pltpu.CompilerParams(
-            collective_id=0, has_side_effects=True, vmem_limit_bytes=60 * 2**20
+            collective_id=0, has_side_effects=True, vmem_limit_bytes=52 * 2**20
         ),
     )(
+        *(pltpu.with_memory_space_constraint(array, pltpu.HBM) for array in (
         fold(payload[0], (SIDE, SIDE, 2, LINES, 128)),
         jnp.transpose(block_scale[0], (2, 1, 0)),
         fold(master, (LINES, 128)),
         fold(moment_one, (LINES, 128)),
         fold(moment_two, (LINES, 128)),
         owner.T,
+        ))
     )
     state = jax.ShapeDtypeStruct((ROWS, TILES, 2, 128), F32)
     results = pl.pallas_call(
@@ -445,13 +430,10 @@
         in_specs=[anywhere] * (1 + len(CHUNKS)),
         out_specs=(anywhere,) * 4,
         scratch_shapes=[
-            pltpu.VMEM((3, ROWS, TILES, 2, 128), F32),
-            pltpu.SemaphoreType.DMA,
             pltpu.SemaphoreType.DMA((3,)),
-            pltpu.SemaphoreType.DMA((len(CHUNKS),)),
             pltpu.SemaphoreType.DMA((len(CHUNKS), DEPTH)),
-            *(pltpu.VMEM((DEPTH, 8, n, 2, 128), BF16) for _, n in CHUNKS),
         ],
+        compiler_params=pltpu.CompilerParams(vmem_limit_bytes=8 * 2**20),
     )(
         fresh.reshape(3, ROWS, TILES, 2, 128),
         *(part.reshape(DEPTH, 8, n, 2, 128) for part, (_, n) in zip(arrived, CHUNKS)),

time: 45 us -> 43.5 us (0.967)
  Pallas kernels: 44.3 us -> 42.8 us
    pallas_call x1, Pallas kernels: 2.02 us -> 0.98 us  [body(): pl.pallas_call(finish, out_shape=(state, state, state, jax.ShapeDtypeStru...]
    pallas_call x1, Pallas kernels: 42.3 us -> 41.8 us  [body(): pl.pallas_call(kernel, out_shape=(jax.ShapeDtypeStruct((3, LINES, 128), F...]
where the time goes in v4:
time: 43.5 us; the launch traced here: 43.4 us
  Pallas kernels  42.8 us (98%)
  between operations  0.64 us (1%)
    pallas_call x1, Pallas kernels, body(): pl.pallas_call(kernel, out_shape=(jax.ShapeDtypeStruct((3, LINES, 128), F...  41.8 us
    pallas_call x1, Pallas kernels, body(): pl.pallas_call(finish, out_shape=(state, state, state, jax.ShapeDtypeStru...  0.98 us

profile of v4, /device:TPU:1, one launch (start us, length us, event | category | flops | bytes accessed | tf_op | source)
XLA Modules:
  0.0 43.4 jit_solution(666488747464330761)
XLA Ops:
  0.6 41.8 %shard_map.93 = (f32[3,320,128]{2,1,0:T(8,128)S(1)}, bf16[8,4,40,128]{3,2,1,0:T(8,128)(2,1)S(1)}) custom-call(bf16[4,4,2,320,128]{4,3,2,1,0:T(8,128)(2,1)} %bitcast.40, f32[10,2,512]{2,1,0:T(2,128)} %bitcast.44, f32[320,128]{1,0:T(8,128)} %bitcast.41, f32[320,128]{1,0:T(8,128)} %bitcast.42, f32[320,128]{1,0:T(8,128)} %bitcast.43, s32[1,16]{1,0:T(1,128)} %bitcast.45), custom_call_target="tpu_custom_call" | custom-call | tf_op jit(solution)/shard_map/pallas_call | solution.py:404
  42.4 1.0 %shard_map.94 = (f32[16,10,2,128]{3,2,1,0:T(2,128)}, f32[16,10,2,128]{3,2,1,0:T(2,128)}, f32[16,10,2,128]{3,2,1,0:T(2,128)}, bf16[8,80,2,128]{3,2,1,0:T(2,128)(2,1)}) custom-call(f32[3,16,10,2,128]{4,3,2,1,0:T(2,128)S(1)} %bitcast.38, bf16[8,8,10,2,128]{4,3,2,1,0:T(2,128)(2,1)S(1)} %bitcast.39), custom_call_target="tpu_custom_call" | custom-call | tf_op jit(solution)/shard_map/pallas_call | solution.py:427

commit v5 on v4

--- a/solution.py
+++ b/solution.py
@@ -21,7 +21,7 @@
 BF16 = jnp.bfloat16
 F32 = jnp.float32
 GROUPS = (0, 1)
-CHUNKS = ((0, 10),)
+CHUNKS = ((0, 4), (4, 6))
 OFFSETS = (2, 1, 3, 0)
 AWAY = sorted(
     ((i, j, core) for i in range(SIDE) for j in range(SIDE) for core in range(2) if (i, j, core) != (0, 0, 0)),
@@ -309,7 +309,7 @@
         master, one, two = (r.state[i, lines] for i in range(3))
         one = 0.9 * one + 0.1 * grad
         two = 0.95 * two + 0.05 * grad * grad
-        direction = one / fix_one / (jnp.sqrt(two / fix_two) + 1e-08)
+        direction = one * (1.0 / fix_one) / (jnp.sqrt(two * (1.0 / fix_two)) + 1e-08)
         master = master - 0.00015 * (direction + 0.1 * master)
         for i, value in enumerate((master, one, two)):
             r.fresh[i, lines] = value

time: 43.5 us -> 43.3 us (level)
  no operation moved by 1% of the time
where the time goes in v5:
time: 43.3 us; the launch traced here: 43.2 us
  Pallas kernels  42.5 us (98%)
  between operations  0.64 us (1%)
    pallas_call x1, Pallas kernels, body(): pl.pallas_call(kernel, out_shape=(jax.ShapeDtypeStruct((3, LINES, 128), F...  41.5 us
    pallas_call x1, Pallas kernels, body(): pl.pallas_call(finish, out_shape=(state, state, state, jax.ShapeDtypeStru...  1.05 us

profile of v5, /device:TPU:1, one launch (start us, length us, event | category | flops | bytes accessed | tf_op | source)
XLA Modules:
  0.0 43.2 jit_solution(12297917217072483159)
XLA Ops:
  0.6 41.5 %shard_map.93 = (f32[3,320,128]{2,1,0:T(8,128)S(1)}, bf16[8,4,16,128]{3,2,1,0:T(8,128)(2,1)S(1)}, bf16[8,4,24,128]{3,2,1,0:T(8,128)(2,1)S(1)}) custom-call(bf16[4,4,2,320,128]{4,3,2,1,0:T(8,128)(2,1)} %bitcast.42, f32[10,2,512]{2,1,0:T(2,128)} %bitcast.46, f32[320,128]{1,0:T(8,128)} %bitcast.43, f32[320,128]{1,0:T(8,128)} %bitcast.44, f32[320,128]{1,0:T(8,128)} %bitcast.45, ...), custom_call_target="tpu_custom_call" | custom-call | tf_op jit(solution)/shard_map/pallas_call | solution.py:404
  42.1 1.1 %shard_map.94 = (f32[16,10,2,128]{3,2,1,0:T(2,128)}, f32[16,10,2,128]{3,2,1,0:T(2,128)}, f32[16,10,2,128]{3,2,1,0:T(2,128)}, bf16[8,80,2,128]{3,2,1,0:T(2,128)(2,1)}) custom-call(f32[3,16,10,2,128]{4,3,2,1,0:T(2,128)S(1)} %bitcast.39, bf16[8,8,4,2,128]{4,3,2,1,0:T(2,128)(2,1)S(1)} %bitcast.41, bf16[8,8,6,2,128]{4,3,2,1,0:T(2,128)(2,1)S(1)} %bitcast.40), custom_call_target="tpu_custom_call" | custom-call | tf_op jit(solution)/shard_map/pallas_call | solution.py:427
